TPU v7x, 128 devices: a whole 4x4x4 slice. The times are simulated.
128 devices in a mesh: kpt: 16 (over z, y_hi, core), row: 8 (over x, y_lo).
Axes of the slice: x: 4, y: 4 (y_hi: 2, y_lo: 2; y = y_hi * 2 + y_lo), z: 4, core: 2. Of those that a mesh axis runs over, the one named last changes fastest.
Arguments:
- occ_orbitals: bfloat16 [64, 2048, 128], P('kpt', 'row'), may hold values from -0.5 to 0.5
- virt_orbitals: bfloat16 [64, 2048, 256], P('kpt', 'row'), may hold values from -0.375 to 0.375
- occ_gap: bfloat16 [64, 128], P('kpt'), may hold values from 0.049804688 to 3
- virt_gap: bfloat16 [64, 256], P('kpt'), may hold values from 0.049804688 to 3
- partner: int32 [3, 64], replicated, may hold values from 0 to 63, as said below
Outputs:
- chi: float32 [3, 4, 2048, 2048], P(None, None, 'row', 'kpt')
Inputs may be any that keep to these rules, and one draw needn't show every extreme that they name: For each transfer q there is a shift s_q of 0 to 4 with partner[q, k] = (k - s_q) mod 64 for every k; the shifts of different transfers differ, and some transfer has s_q = 4.
All inputs are finite; a program needn't handle non-finite values.
Results may differ from a plain program's by a relative error of at most 0.0003.
Values may be sent and summed in bfloat16 or wider, within the bound.
No kernel may reach another device: no remote copies, remote signals or barrier semaphores. Data moves between devices by JAX's collectives and lax.ppermute only.
A program may use at most 320 MiB of HBM per device.

v0:
```python
import jax
import jax.numpy as jnp
from jax import lax
from jax.sharding import PartitionSpec as P

NTAU = 4


def shifted(block, axis, distance):
    devices = range(lax.axis_size(axis))
    route = [((i - distance) % len(devices), i) for i in devices]
    return lax.ppermute(block, axis, route)


def weighted(orbitals, energy_gap, moment):
    factor = jnp.exp(-energy_gap.astype(jnp.float32) * moment)
    return (orbitals.astype(jnp.float32) * factor[:, None, :]).astype(jnp.bfloat16)


def greens(row_panel, column_panel):
    return jnp.einsum("kri,kci->krc", row_panel, column_panel, preferred_element_type=jnp.float32)


def on_device(occ_orbitals, virt_orbitals, occ_gap, virt_gap, partner):
    local_count = occ_orbitals.shape[0]
    transfers = partner.shape[0]
    device_k = lax.axis_index("kpt")
    kpt_count = lax.axis_size("kpt")
    total_count = local_count * kpt_count
    tau_values = 0.25 * 2.0 ** jnp.arange(NTAU, dtype=jnp.float32)
    earlier, earlier_gap = shifted((virt_orbitals, virt_gap), "kpt", 1)
    window = jnp.concatenate([earlier, virt_orbitals], axis=0)
    window_gap = jnp.concatenate([earlier_gap, virt_gap], axis=0)
    occ_points, window_points = (
        lax.all_gather(occ_orbitals, "row", axis=1, tiled=True),
        lax.all_gather(window, "row", axis=1, tiled=True),
    )
    window_start = (device_k - 1) % kpt_count * local_count
    own_partners = lax.dynamic_slice_in_dim(partner, device_k * local_count, local_count, 1)
    window_slots = (own_partners - window_start) % total_count
    blocks = []
    for step_index in range(NTAU):
        moment = tau_values[step_index]
        occ_green = greens(weighted(occ_orbitals, occ_gap, moment), occ_points)
        window_green = greens(weighted(window, window_gap, moment), window_points)
        sums_here = []
        for transfer in range(transfers):
            virt_green = jnp.take(window_green, window_slots[transfer], axis=0)
            sums_here.append(jnp.sum(occ_green * virt_green, axis=0))
        blocks.append(jnp.stack(sums_here))
    partial_chi = jnp.stack(blocks, axis=1)
    return lax.psum_scatter(partial_chi, "kpt", scatter_dimension=3, tiled=True)


def solution(mesh):
    in_specs = (P("kpt", "row", None), P("kpt", "row", None), P("kpt", None), P("kpt", None), P())
    out_specs = P(None, None, "row", "kpt")
    return jax.shard_map(
        on_device, mesh=mesh, in_specs=in_specs, out_specs=out_specs, check_vma=False
    )
```

profile of v0, /device:TPU:0, one launch (start us, length us, event | category | flops | bytes accessed | tf_op | source)
XLA Modules:
  0.0 672.6 jit_solution(10902497259233163905)
XLA Ops:
  6.5 0.0 all-gather.3.cloned.1.call-start
  6.5 0.7 all-gather.3.cloned.1.call-update
  7.3 0.0 all-gather.5.cloned.1.call-start
  7.3 0.1 collective-permute-start
  7.4 13.3 %collective-permute-done = bf16[4,256,256]{2,1,0:T(8,128)(2,1)S(1)} collective-permute-done((bf16[4,256,256]{2,1,0:T(8,128)(2,1)}, bf16[4,256,256]{2,1,0:T(8,128)(2,1)S(1)}, u32[]{:S(2)}, u32[]{:S(2)}) %collective-permute-start) | collective-permute-done | bytes 524320 | tf_op jit(solution)/shard_map/ppermute | solution.py:12
  20.7 1.1 constant_dynamic-update-slice_fusion
  21.8 0.0 copy-start
  21.8 1.0 copy-done
  22.7 0.0 all-gather.5.cloned.1.call-update
  22.8 0.0 reduce-scatter.2.cloned.1.call-start
  22.8 0.1 collective-permute-start.1
  22.9 0.8 add_select_fusion
  23.7 0.6 fusion.45
  24.3 3.1 multiply_exponential_fusion.5
  27.4 2.3 collective-permute-done.1
  29.7 3.1 multiply_exponential_fusion.1
  32.8 29.8 %all-gather.3.cloned.1.call-done = bf16[4,2048,128]{2,1,0:T(8,128)(2,1)} async-done(((bf16[4,256,128]{2,1,0:T(8,128)(2,1)}), bf16[4,2048,128]{2,1,0:T(8,128)(2,1)}) %all-gather.3.cloned.1.call-update) | async-done | bytes 2097168 | tf_op jit(solution)/shard_map/all_gather | solution.py:35
  62.6 0.0 copy-start.2
  62.6 6.3 fusion.34
  68.9 0.0 copy-done.10
  68.9 0.0 copy-done.2
  68.9 4.5 fusion.36
  73.4 0.0 copy-start.1
  73.4 4.5 fusion.32
  77.8 4.5 fusion.38
  82.3 151.1 %all-gather.5.cloned.1.call-done = bf16[8,2048,256]{2,1,0:T(8,128)(2,1)} async-done(((bf16[8,256,256]{2,1,0:T(8,128)(2,1)}), bf16[8,2048,256]{2,1,0:T(8,128)(2,1)}) %all-gather.5.cloned.1.call-update) | async-done | bytes 8388624 | tf_op jit(solution)/shard_map/all_gather | solution.py:36
  233.3 0.0 copy-done.1
  233.3 11.5 %fusion.16 = f32[8,256,2048]{2,1,0:T(8,128)} fusion(bf16[8,2048,256]{2,1,0:T(8,128)(2,1)} %all-gather.5.cloned.1.call-done, bf16[8,256,256]{2,1,0:T(8,128)(2,1)S(1)} %copy-done.1, f32[8,256]{1,0:T(8,128)S(1)} %get-tuple-element.34), kind=kOutput, calls=%fused_computation.49 | convolution fusion | flops 2149056512 | bytes 26222592 | tf_op jit(solution)/shard_map/kri,kci->krc/dot_general | solution.py:21
  244.8 10.0 %gather_fusion.11 = f32[4,256,2048]{2,1,0:T(8,128)} fusion(f32[8,256,2048]{2,1,0:T(8,128)} %fusion.16, s32[1024]{0:T(1024)S(1)} %get-tuple-element.49), kind=kCustom, calls=%fused_computation.11.clone | custom fusion | bytes 16777232 | tf_op jit(solution)/shard_map/jit(_take)/gather | solution.py:48
  254.9 10.1 %gather_fusion.10 = f32[4,256,2048]{2,1,0:T(8,128)} fusion(f32[8,256,2048]{2,1,0:T(8,128)} %fusion.16, s32[1024]{0:T(1024)S(1)} %get-tuple-element.50), kind=kCustom, calls=%fused_computation.10.clone | custom fusion | bytes 16777232 | tf_op jit(solution)/shard_map/jit(_take)/gather | solution.py:48
  265.0 11.5 %fusion.18 = f32[8,256,2048]{2,1,0:T(8,128)} fusion(bf16[8,2048,256]{2,1,0:T(8,128)(2,1)} %all-gather.5.cloned.1.call-done, bf16[8,256,256]{2,1,0:T(8,128)(2,1)S(1)} %copy-done.1, f32[8,256]{1,0:T(8,128)S(1)} %get-tuple-element.33), kind=kOutput, calls=%fused_computation.50 | convolution fusion | flops 2149056512 | bytes 26222592 | tf_op jit(solution)/shard_map/kri,kci->krc/dot_general | solution.py:21
  276.5 10.1 %gather_fusion.8 = f32[4,256,2048]{2,1,0:T(8,128)} fusion(f32[8,256,2048]{2,1,0:T(8,128)} %fusion.18, s32[1024]{0:T(1024)S(1)} %get-tuple-element.49), kind=kCustom, calls=%fused_computation.8.clone | custom fusion | bytes 16777232 | tf_op jit(solution)/shard_map/jit(_take)/gather | solution.py:48
  286.6 10.3 %gather_fusion.7 = f32[4,256,2048]{2,1,0:T(8,128)} fusion(f32[8,256,2048]{2,1,0:T(8,128)} %fusion.18, s32[1024]{0:T(1024)S(1)} %get-tuple-element.50), kind=kCustom, calls=%fused_computation.7.clone | custom fusion | bytes 16777232 | tf_op jit(solution)/shard_map/jit(_take)/gather | solution.py:48
  296.9 10.0 %gather_fusion.9 = f32[4,256,2048]{2,1,0:T(8,128)} fusion(f32[8,256,2048]{2,1,0:T(8,128)} %fusion.16, s32[1024]{0:T(1024)S(1)} %pad_clamp_fusion.2), kind=kCustom, calls=%fused_computation.9.clone | custom fusion | bytes 16777232 | tf_op jit(solution)/shard_map/jit(_take)/gather | solution.py:48
  307.0 10.0 %gather_fusion.6 = f32[4,256,2048]{2,1,0:T(8,128)} fusion(f32[8,256,2048]{2,1,0:T(8,128)} %fusion.18, s32[1024]{0:T(1024)S(1)} %pad_clamp_fusion.2), kind=kCustom, calls=%fused_computation.6.clone | custom fusion | bytes 16777232 | tf_op jit(solution)/shard_map/jit(_take)/gather | solution.py:48
  317.0 11.5 %fusion.22 = f32[8,256,2048]{2,1,0:T(8,128)} fusion(bf16[8,2048,256]{2,1,0:T(8,128)(2,1)} %all-gather.5.cloned.1.call-done, bf16[8,256,256]{2,1,0:T(8,128)(2,1)S(1)} %copy-done.1, f32[8,256]{1,0:T(8,128)S(1)} %get-tuple-element.36), kind=kOutput, calls=%fused_computation.52 | convolution fusion | flops 2149056512 | bytes 26222592 | tf_op jit(solution)/shard_map/kri,kci->krc/dot_general | solution.py:21
  328.5 10.1 %gather_fusion.2 = f32[4,256,2048]{2,1,0:T(8,128)} fusion(f32[8,256,2048]{2,1,0:T(8,128)} %fusion.22, s32[1024]{0:T(1024)S(1)} %get-tuple-element.49), kind=kCustom, calls=%fused_computation.2.clone | custom fusion | bytes 16777232 | tf_op jit(solution)/shard_map/jit(_take)/gather | solution.py:48
  338.6 10.1 %gather_fusion.1 = f32[4,256,2048]{2,1,0:T(8,128)} fusion(f32[8,256,2048]{2,1,0:T(8,128)} %fusion.22, s32[1024]{0:T(1024)S(1)} %get-tuple-element.50), kind=kCustom, calls=%fused_computation.1.clone | custom fusion | bytes 16777232 | tf_op jit(solution)/shard_map/jit(_take)/gather | solution.py:48
  348.6 10.1 %gather_fusion = f32[4,256,2048]{2,1,0:T(8,128)} fusion(f32[8,256,2048]{2,1,0:T(8,128)} %fusion.22, s32[1024]{0:T(1024)S(1)} %pad_clamp_fusion.2), kind=kCustom, calls=%fused_computation.clone | custom fusion | bytes 16777232 | tf_op jit(solution)/shard_map/jit(_take)/gather | solution.py:48
  358.8 11.5 %fusion.20 = f32[8,256,2048]{2,1,0:T(8,128)} fusion(bf16[8,2048,256]{2,1,0:T(8,128)(2,1)} %all-gather.5.cloned.1.call-done, bf16[8,256,256]{2,1,0:T(8,128)(2,1)S(1)} %copy-done.1, f32[8,256]{1,0:T(8,128)S(1)} %get-tuple-element.35), kind=kOutput, calls=%fused_computation.51 | convolution fusion | flops 2149056512 | bytes 26222592 | tf_op jit(solution)/shard_map/kri,kci->krc/dot_general | solution.py:21
  370.3 10.1 %gather_fusion.5 = f32[4,256,2048]{2,1,0:T(8,128)} fusion(f32[8,256,2048]{2,1,0:T(8,128)} %fusion.20, s32[1024]{0:T(1024)S(1)} %get-tuple-element.49), kind=kCustom, calls=%fused_computation.5.clone | custom fusion | bytes 16777232 | tf_op jit(solution)/shard_map/jit(_take)/gather | solution.py:48
  380.3 10.1 %gather_fusion.3 = f32[4,256,2048]{2,1,0:T(8,128)} fusion(f32[8,256,2048]{2,1,0:T(8,128)} %fusion.20, s32[1024]{0:T(1024)S(1)} %pad_clamp_fusion.2), kind=kCustom, calls=%fused_computation.3.clone | custom fusion | bytes 16777232 | tf_op jit(solution)/shard_map/jit(_take)/gather | solution.py:48
  390.4 10.0 %gather_fusion.4 = f32[4,256,2048]{2,1,0:T(8,128)} fusion(f32[8,256,2048]{2,1,0:T(8,128)} %fusion.20, s32[1024]{0:T(1024)S(1)} %get-tuple-element.50), kind=kCustom, calls=%fused_computation.4.clone | custom fusion | bytes 16777232 | tf_op jit(solution)/shard_map/jit(_take)/gather | solution.py:48
  400.5 51.4 %fusion.2 = (f32[256,2048]{1,0:T(8,128)}, f32[256,2048]{1,0:T(8,128)}, f32[256,2048]{1,0:T(8,128)}, f32[256,2048]{1,0:T(8,128)}, f32[256,2048]{1,0:T(8,128)}, /*...) fusion(f32[4,256,2048]{2,1,0:T(8,128)} %fusion.32, ...), kind=kLoop, calls=%fused_computation.18 | loop fusion | flops 69206016 | bytes 159383568 | tf_op jit(solution)/shard_map/reduce_sum | solution.py:49
  451.8 0.0 copy-start.7
  451.8 0.0 copy-start.8
  451.8 3.4 maximum_bitcast_fusion.3
  455.3 0.0 copy-start.4
  455.3 0.0 copy-start.5
  455.3 0.0 copy-start.6
  455.3 0.0 copy-done.7
  455.3 0.6 copy-done.8
  455.9 0.6 copy-done.9
  456.6 0.8 maximum_bitcast_fusion
  457.3 0.0 copy-start.3
  457.4 0.0 copy-done.4
  457.4 0.6 copy-done.5
  458.0 0.6 copy-done.6
  458.6 0.8 maximum_bitcast_fusion.1
  459.4 0.0 copy-done.3
  459.4 2.1 maximum_bitcast_fusion.2
  461.5 8.5 %pad_maximum_fusion = f32[3,4,256,2048]{3,2,1,0:T(8,128)} fusion(f32[3,1,256,2048]{3,2,1,0:T(8,128)S(1)} %maximum_bitcast_fusion.3, f32[3,1,256,2048]{3,2,1,0:T(8,128)S(1)} %maximum_bitcast_fusion.2, f32[3,1,256,2048]{3,2,1,0:T(8,128)S(1)} %maximum_bitcast_fusion.1, f32[3,1,256,2048]{3,2,1,0:T(8,128)S(1)} %maximum_bitcast_fusion), kind=kLoop, calls=%fused_computation.12 | loop fusion | flops 18874368 | bytes 50331648 | tf_op jit(solution)/shard_map/stack | solution.py:51
  470.0 0.0 reduce-scatter.2.cloned.1.call-update
  470.1 196.0 %reduce-scatter.2.cloned.1.call-done = f32[3,4,256,128]{3,2,1,0:T(8,128)} async-done(((f32[3,4,256,2048]{3,2,1,0:T(8,128)}), f32[3,4,256,128]{3,2,1,0:T(8,128)}) %reduce-scatter.2.cloned.1.call-update) | async-done | bytes 1572880 | tf_op jit(solution)/shard_map/reduce_scatter | solution.py:52
  (7 shorter events, 0.1 us)
Async XLA Ops:
  6.5 62.4 %copy-start.10 = (bf16[4,256,128]{2,1,0:T(8,128)(2,1)S(1)}, bf16[4,256,128]{2,1,0:T(8,128)(2,1)}, u32[]{:S(2)}) copy-start(bf16[4,256,128]{2,1,0:T(8,128)(2,1)} %param.7) | copy-start | bytes 786436
  6.5 56.1 %all-gather.3.cloned.1.call-start = ((), (), s32[]{:S(2)}) async-start(), calls=%async_computation.1 | async-start | bytes 2359296 | tf_op jit(solution)/shard_map/all_gather | solution.py:35
  7.3 226.1 %all-gather.5.cloned.1.call-start = ((), (), s32[]{:S(2)}) async-start(), calls=%async_computation.2 | async-start | bytes 9437184 | tf_op jit(solution)/shard_map/all_gather | solution.py:36
  7.3 13.3 %collective-permute-start = (bf16[4,256,256]{2,1,0:T(8,128)(2,1)}, bf16[4,256,256]{2,1,0:T(8,128)(2,1)S(1)}, u32[]{:S(2)}, u32[]{:S(2)}) collective-permute-start(bf16[4,256,256]{2,1,0:T(8,128)(2,1)} %param.8), channel_id=1, source_target_pairs={{120,0},{0,8},{8,16},{16,24},{24,32},{32,40},{40,48},{48,56},{56,6... | collective-permute-start | bytes 1572872 | tf_op jit(solution)/shard_map/ppermute | solution.py:12
  21.8 1.0 copy-start
  22.8 643.3 %reduce-scatter.2.cloned.1.call-start = ((), (), s32[]{:S(2)}) async-start(), calls=%async_computation.3 | async-start | bytes 26738688 | tf_op jit(solution)/shard_map/reduce_scatter | solution.py:52
  22.8 6.9 %collective-permute-start.1 = (bf16[4,256]{1,0:T(4,128)(2,1)}, bf16[4,256]{1,0:T(4,128)(2,1)S(1)}, u32[]{:S(2)}, u32[]{:S(2)}) collective-permute-start(bf16[4,256]{1,0:T(4,128)(2,1)} %param.10), channel_id=1, source_target_pairs={{120,0},{0,8},{8,16},{16,24},{24,32},{32,40},{40,48},{48,56},{56,6... | collective-permute-start | bytes 6152 | tf_op jit(solution)/shard_map/ppermute | solution.py:12
  62.6 6.3 copy-start.2
  73.4 160.0 %copy-start.1 = (bf16[8,256,256]{2,1,0:T(8,128)(2,1)S(1)}, bf16[8,256,256]{2,1,0:T(8,128)(2,1)}, u32[]{:S(2)}) copy-start(bf16[8,256,256]{2,1,0:T(8,128)(2,1)} %copy-done) | copy-start | bytes 3145732
  451.8 3.5 copy-start.7
  451.8 4.1 copy-start.8
  451.8 4.7 copy-start.9
  455.3 2.1 copy-start.4
  455.3 2.7 copy-start.5
  455.3 3.3 copy-start.6
  457.3 2.0 copy-start.3
Sparse Core Ops, SparseCore 0:
  9.0 53.5 all-gather.2
  64.3 169.0 all-gather.4
  470.2 195.8 reduce-scatter.1
where the time goes:
time: 674 us; the launch traced here: 673 us
  waiting for transfers between devices  393 us (58%)
  local copies, waits for them, and re-layouts  126 us (19%)
  other arithmetic  74 us (11%)
  matrix products  65.6 us (10%)
  between operations  13.3 us (2%)
    reduce_scatter x1, waiting for transfers between devices, on_device(): return lax.psum_scatter(partial_chi, 'kpt', scatter_dimension=3, tiled=True)  196 us
    all_gather x1, waiting for transfers between devices, on_device(): lax.all_gather(window, 'row', axis=1, tiled=True)  151 us
    gather x12, local copies, waits for them, and re-layouts, on_device(): virt_green = jnp.take(window_green, window_slots[transfer], axis=0)  121 us
    dot_general x8, matrix products, greens(): jnp.einsum('kri,kci->krc', row_panel, column_panel, preferred_element_typ...  65.6 us
    reduce_sum x1, other arithmetic, on_device(): sums_here.append(jnp.sum(occ_green * virt_green, axis=0))  51.4 us
    all_gather x1, waiting for transfers between devices, on_device(): lax.all_gather(occ_orbitals, 'row', axis=1, tiled=True)  29.8 us
    another operation x5, other arithmetic, on_device(): partial_chi = jnp.stack(blocks, axis=1)  15.6 us
    ppermute x2, waiting for transfers between devices, shifted(): return lax.ppermute(block, axis, route)  15.6 us
  transfers between devices with their start and end apart: 5, of which 5 were waited for; matrix products, arithmetic and copies ran while one was open for 4% of the time, Pallas kernels for 0%

commit v1 on v0

--- a/solution.py
+++ b/solution.py
@@ -33,7 +33,9 @@
     window_gap = jnp.concatenate([earlier_gap, virt_gap], axis=0)
     occ_points, window_points = (
         lax.all_gather(occ_orbitals, "row", axis=1, tiled=True),
-        lax.all_gather(window, "row", axis=1, tiled=True),
+        jnp.concatenate(
+            lax.all_to_all(jnp.stack([window] * lax.axis_size("row")), "row", 0, 0), axis=1
+        ),
     )
     window_start = (device_k - 1) % kpt_count * local_count
     own_partners = lax.dynamic_slice_in_dim(partner, device_k * local_count, local_count, 1)

time: 674 us -> 626 us (0.929)
  waiting for transfers between devices: 393 us -> 332 us
  local copies, waits for them, and re-layouts: 126 us -> 137 us
    all_gather x1 -> x0, waiting for transfers between devices: 151 us -> none  [on_device(): lax.all_gather(window, 'row', axis=1, tiled=True)]
    ppermute x2, waiting for transfers between devices: 15.6 us -> 114 us  [shifted(): return lax.ppermute(block, axis, route)]
    reshape x0 -> x1, local copies, waits for them, and re-layouts: none -> 7.57 us  [on_device(): jnp.concatenate(lax.all_to_all(jnp.stack([window] * lax.axis_size('row'))...]
  transfers between devices with their start and end apart: 5 -> 5, of which waited for: 5 -> 4; matrix products, arithmetic and copies ran while one was open for 4% -> 4% of each run, Pallas kernels for 0% -> 0%
where the time goes in v1:
time: 626 us; the launch traced here: 625 us
  waiting for transfers between devices  332 us (53%)
  local copies, waits for them, and re-layouts  137 us (22%)
  other arithmetic  72 us (12%)
  matrix products  65.5 us (10%)
  between operations  13.6 us (2%)
    reduce_scatter x1, waiting for transfers between devices, on_device(): return lax.psum_scatter(partial_chi, 'kpt', scatter_dimension=3, tiled=True)  192 us
    gather x12, local copies, waits for them, and re-layouts, on_device(): virt_green = jnp.take(window_green, window_slots[transfer], axis=0)  121 us
    ppermute x2, waiting for transfers between devices, shifted(): return lax.ppermute(block, axis, route)  114 us
    dot_general x8, matrix products, greens(): jnp.einsum('kri,kci->krc', row_panel, column_panel, preferred_element_typ...  65.5 us
    reduce_sum x1, other arithmetic, on_device(): sums_here.append(jnp.sum(occ_green * virt_green, axis=0))  51.4 us
    all_gather x1, waiting for transfers between devices, on_device(): lax.all_gather(occ_orbitals, 'row', axis=1, tiled=True)  25 us
    another operation x5, other arithmetic, on_device(): partial_chi = jnp.stack(blocks, axis=1)  15.6 us
  transfers between devices with their start and end apart: 5, of which 4 were waited for; matrix products, arithmetic and copies ran while one was open for 4% of the time, Pallas kernels for 0%

profile of v1, /device:TPU:0, one launch (start us, length us, event | category | flops | bytes accessed | tf_op | source)
XLA Modules:
  0.0 625.1 jit_solution(5882490920319735921)
XLA Ops:
  6.5 0.0 collective-permute-start
  6.5 13.3 %collective-permute-done = bf16[4,256,256]{2,1,0:T(8,128)(2,1)S(1)} collective-permute-done((bf16[4,256,256]{2,1,0:T(8,128)(2,1)}, bf16[4,256,256]{2,1,0:T(8,128)(2,1)S(1)}, u32[]{:S(2)}, u32[]{:S(2)}) %collective-permute-start) | collective-permute-done | bytes 524320 | tf_op jit(solution)/shard_map/ppermute | solution.py:12
  19.8 1.1 constant_dynamic-update-slice_fusion
  20.9 4.2 stack.74
  25.1 0.0 copy-start.9
  25.2 0.0 copy-start.10
  25.2 0.0 copy-start.11
  25.2 5.1 all-to-all-start
  30.3 0.0 all-gather.2.cloned.1.call-start
  30.3 0.7 all-gather.2.cloned.1.call-update
  31.0 0.0 reduce-scatter.2.cloned.1.call-start
  31.1 0.0 copy-done.9
  31.1 0.1 collective-permute-start.1
  31.2 0.0 copy-done.10
  31.2 0.1 add_select_fusion
  31.3 0.6 fusion.45
  31.9 0.0 copy-done.11
  31.9 2.4 multiply_exponential_fusion.5
  34.4 100.2 %collective-permute-done.1 = bf16[4,256]{1,0:T(4,128)(2,1)S(1)} collective-permute-done((bf16[4,256]{1,0:T(4,128)(2,1)S(1)}, bf16[4,256]{1,0:T(4,128)(2,1)S(1)}, u32[]{:S(2)}, u32[]{:S(2)}) %collective-permute-start.1) | collective-permute-done | bytes 2080 | tf_op jit(solution)/shard_map/ppermute | solution.py:12
  134.6 2.4 multiply_exponential_fusion.1
  137.1 25.0 %all-gather.2.cloned.1.call-done = bf16[4,2048,128]{2,1,0:T(8,128)(2,1)} async-done(((bf16[4,256,128]{2,1,0:T(8,128)(2,1)}), bf16[4,2048,128]{2,1,0:T(8,128)(2,1)}) %all-gather.2.cloned.1.call-update) | async-done | bytes 2097168 | tf_op jit(solution)/shard_map/all_gather | solution.py:35
  162.0 0.0 copy-done.8
  162.0 6.2 fusion.34
  168.2 0.0 copy-done
  168.2 4.5 fusion.36
  172.7 4.5 fusion.32
  177.1 4.5 fusion.38
  181.6 0.0 all-to-all-done
  181.6 7.6 %copy.6 = bf16[8,8,256,256]{3,2,1,0:T(8,128)(2,1)} copy(bf16[8,8,256,256]{3,2,0,1:T(8,128)(2,1)} %bitcast.2) | data formatting | bytes 16777216 | tf_op jit(solution)/shard_map/reshape | solution.py:36
  189.2 11.5 %fusion.16 = f32[8,256,2048]{2,1,0:T(8,128)} fusion(bf16[8,2048,256]{2,1,0:T(8,128)(2,1)} %bitcast.43, bf16[8,256,256]{2,1,0:T(8,128)(2,1)S(1)} %constant_dynamic-update-slice_fusion, f32[8,256]{1,0:T(8,128)S(1)} %get-tuple-element.34), kind=kOutput, calls=%fused_computation.49 | convolution fusion | flops 2149056512 | bytes 26222592 | tf_op jit(solution)/shard_map/kri,kci->krc/dot_general | solution.py:21
  200.7 10.0 %gather_fusion.11 = f32[4,256,2048]{2,1,0:T(8,128)} fusion(f32[8,256,2048]{2,1,0:T(8,128)} %fusion.16, s32[1024]{0:T(1024)S(1)} %get-tuple-element.49), kind=kCustom, calls=%fused_computation.11.clone | custom fusion | bytes 16777232 | tf_op jit(solution)/shard_map/jit(_take)/gather | solution.py:50
  210.7 10.1 %gather_fusion.10 = f32[4,256,2048]{2,1,0:T(8,128)} fusion(f32[8,256,2048]{2,1,0:T(8,128)} %fusion.16, s32[1024]{0:T(1024)S(1)} %get-tuple-element.50), kind=kCustom, calls=%fused_computation.10.clone | custom fusion | bytes 16777232 | tf_op jit(solution)/shard_map/jit(_take)/gather | solution.py:50
  220.8 11.5 %fusion.18 = f32[8,256,2048]{2,1,0:T(8,128)} fusion(bf16[8,2048,256]{2,1,0:T(8,128)(2,1)} %bitcast.44, bf16[8,256,256]{2,1,0:T(8,128)(2,1)S(1)} %constant_dynamic-update-slice_fusion, f32[8,256]{1,0:T(8,128)S(1)} %get-tuple-element.33), kind=kOutput, calls=%fused_computation.50 | convolution fusion | flops 2149056512 | bytes 26222592 | tf_op jit(solution)/shard_map/kri,kci->krc/dot_general | solution.py:21
  232.3 10.3 %gather_fusion.8 = f32[4,256,2048]{2,1,0:T(8,128)} fusion(f32[8,256,2048]{2,1,0:T(8,128)} %fusion.18, s32[1024]{0:T(1024)S(1)} %get-tuple-element.49), kind=kCustom, calls=%fused_computation.8.clone | custom fusion | bytes 16777232 | tf_op jit(solution)/shard_map/jit(_take)/gather | solution.py:50
  242.6 10.1 %gather_fusion.7 = f32[4,256,2048]{2,1,0:T(8,128)} fusion(f32[8,256,2048]{2,1,0:T(8,128)} %fusion.18, s32[1024]{0:T(1024)S(1)} %get-tuple-element.50), kind=kCustom, calls=%fused_computation.7.clone | custom fusion | bytes 16777232 | tf_op jit(solution)/shard_map/jit(_take)/gather | solution.py:50
  252.8 10.0 %gather_fusion.9 = f32[4,256,2048]{2,1,0:T(8,128)} fusion(f32[8,256,2048]{2,1,0:T(8,128)} %fusion.16, s32[1024]{0:T(1024)S(1)} %pad_clamp_fusion.2), kind=kCustom, calls=%fused_computation.9.clone | custom fusion | bytes 16777232 | tf_op jit(solution)/shard_map/jit(_take)/gather | solution.py:50
  262.8 10.0 %gather_fusion.6 = f32[4,256,2048]{2,1,0:T(8,128)} fusion(f32[8,256,2048]{2,1,0:T(8,128)} %fusion.18, s32[1024]{0:T(1024)S(1)} %pad_clamp_fusion.2), kind=kCustom, calls=%fused_computation.6.clone | custom fusion | bytes 16777232 | tf_op jit(solution)/shard_map/jit(_take)/gather | solution.py:50
  272.9 11.5 %fusion.22 = f32[8,256,2048]{2,1,0:T(8,128)} fusion(bf16[8,2048,256]{2,1,0:T(8,128)(2,1)} %bitcast.45, bf16[8,256,256]{2,1,0:T(8,128)(2,1)S(1)} %constant_dynamic-update-slice_fusion, f32[8,256]{1,0:T(8,128)S(1)} %get-tuple-element.36), kind=kOutput, calls=%fused_computation.52 | convolution fusion | flops 2149056512 | bytes 26222592 | tf_op jit(solution)/shard_map/kri,kci->krc/dot_general | solution.py:21
  284.4 10.1 %gather_fusion.2 = f32[4,256,2048]{2,1,0:T(8,128)} fusion(f32[8,256,2048]{2,1,0:T(8,128)} %fusion.22, s32[1024]{0:T(1024)S(1)} %get-tuple-element.49), kind=kCustom, calls=%fused_computation.2.clone | custom fusion | bytes 16777232 | tf_op jit(solution)/shard_map/jit(_take)/gather | solution.py:50
  294.4 10.1 %gather_fusion.1 = f32[4,256,2048]{2,1,0:T(8,128)} fusion(f32[8,256,2048]{2,1,0:T(8,128)} %fusion.22, s32[1024]{0:T(1024)S(1)} %get-tuple-element.50), kind=kCustom, calls=%fused_computation.1.clone | custom fusion | bytes 16777232 | tf_op jit(solution)/shard_map/jit(_take)/gather | solution.py:50
  304.5 10.1 %gather_fusion = f32[4,256,2048]{2,1,0:T(8,128)} fusion(f32[8,256,2048]{2,1,0:T(8,128)} %fusion.22, s32[1024]{0:T(1024)S(1)} %pad_clamp_fusion.2), kind=kCustom, calls=%fused_computation.clone | custom fusion | bytes 16777232 | tf_op jit(solution)/shard_map/jit(_take)/gather | solution.py:50
  314.6 11.5 %fusion.20 = f32[8,256,2048]{2,1,0:T(8,128)} fusion(bf16[8,2048,256]{2,1,0:T(8,128)(2,1)} %bitcast.46, bf16[8,256,256]{2,1,0:T(8,128)(2,1)S(1)} %constant_dynamic-update-slice_fusion, f32[8,256]{1,0:T(8,128)S(1)} %get-tuple-element.35), kind=kOutput, calls=%fused_computation.51 | convolution fusion | flops 2149056512 | bytes 26222592 | tf_op jit(solution)/shard_map/kri,kci->krc/dot_general | solution.py:21
  326.1 10.1 %gather_fusion.5 = f32[4,256,2048]{2,1,0:T(8,128)} fusion(f32[8,256,2048]{2,1,0:T(8,128)} %fusion.20, s32[1024]{0:T(1024)S(1)} %get-tuple-element.49), kind=kCustom, calls=%fused_computation.5.clone | custom fusion | bytes 16777232 | tf_op jit(solution)/shard_map/jit(_take)/gather | solution.py:50
  336.2 10.1 %gather_fusion.3 = f32[4,256,2048]{2,1,0:T(8,128)} fusion(f32[8,256,2048]{2,1,0:T(8,128)} %fusion.20, s32[1024]{0:T(1024)S(1)} %pad_clamp_fusion.2), kind=kCustom, calls=%fused_computation.3.clone | custom fusion | bytes 16777232 | tf_op jit(solution)/shard_map/jit(_take)/gather | solution.py:50
  346.2 10.0 %gather_fusion.4 = f32[4,256,2048]{2,1,0:T(8,128)} fusion(f32[8,256,2048]{2,1,0:T(8,128)} %fusion.20, s32[1024]{0:T(1024)S(1)} %get-tuple-element.50), kind=kCustom, calls=%fused_computation.4.clone | custom fusion | bytes 16777232 | tf_op jit(solution)/shard_map/jit(_take)/gather | solution.py:50
  356.3 51.4 %fusion.2 = (f32[256,2048]{1,0:T(8,128)}, f32[256,2048]{1,0:T(8,128)}, f32[256,2048]{1,0:T(8,128)}, f32[256,2048]{1,0:T(8,128)}, f32[256,2048]{1,0:T(8,128)}, /*...) fusion(f32[4,256,2048]{2,1,0:T(8,128)} %fusion.32, ...), kind=kLoop, calls=%fused_computation.18 | loop fusion | flops 69206016 | bytes 159383568 | tf_op jit(solution)/shard_map/reduce_sum | solution.py:51
  407.7 3.4 maximum_bitcast_fusion.3
  411.1 0.0 copy-start.2
  411.1 0.0 copy-start.3
  411.1 0.0 copy-start.4
  411.1 0.0 copy-done.5
  411.2 0.6 copy-done.6
  411.8 0.6 copy-done.7
  412.4 0.8 maximum_bitcast_fusion
  413.2 0.0 copy-start.1
  413.2 0.0 copy-done.2
  413.2 0.6 copy-done.3
  413.8 0.6 copy-done.4
  414.4 0.8 maximum_bitcast_fusion.1
  415.2 0.0 copy-done.1
  415.2 2.1 maximum_bitcast_fusion.2
  417.4 8.5 %pad_maximum_fusion = f32[3,4,256,2048]{3,2,1,0:T(8,128)} fusion(f32[3,1,256,2048]{3,2,1,0:T(8,128)S(1)} %maximum_bitcast_fusion.3, f32[3,1,256,2048]{3,2,1,0:T(8,128)S(1)} %maximum_bitcast_fusion.2, f32[3,1,256,2048]{3,2,1,0:T(8,128)S(1)} %maximum_bitcast_fusion.1, f32[3,1,256,2048]{3,2,1,0:T(8,128)S(1)} %maximum_bitcast_fusion), kind=kLoop, calls=%fused_computation.12 | loop fusion | flops 18874368 | bytes 50331648 | tf_op jit(solution)/shard_map/stack | solution.py:53
  425.9 0.0 reduce-scatter.2.cloned.1.call-update
  425.9 192.4 %reduce-scatter.2.cloned.1.call-done = f32[3,4,256,128]{3,2,1,0:T(8,128)} async-done(((f32[3,4,256,2048]{3,2,1,0:T(8,128)}), f32[3,4,256,128]{3,2,1,0:T(8,128)}) %reduce-scatter.2.cloned.1.call-update) | async-done | bytes 1572880 | tf_op jit(solution)/shard_map/reduce_scatter | solution.py:54
  (10 shorter events, 0.1 us)
Async XLA Ops:
  6.5 13.3 %collective-permute-start = (bf16[4,256,256]{2,1,0:T(8,128)(2,1)}, bf16[4,256,256]{2,1,0:T(8,128)(2,1)S(1)}, u32[]{:S(2)}, u32[]{:S(2)}) collective-permute-start(bf16[4,256,256]{2,1,0:T(8,128)(2,1)} %param.8), channel_id=1, source_target_pairs={{120,0},{0,8},{8,16},{16,24},{24,32},{32,40},{40,48},{48,56},{56,6... | collective-permute-start | bytes 1572872 | tf_op jit(solution)/shard_map/ppermute | solution.py:12
  25.1 5.9 copy-start.9
  25.2 6.0 copy-start.10
  25.2 6.8 %copy-start.11 = (bf16[4,128]{1,0:T(4,128)(2,1)S(1)}, bf16[4,128]{1,0:T(4,128)(2,1)}, u32[]{:S(2)}) copy-start(bf16[4,128]{1,0:T(4,128)(2,1)} %param.9) | copy-start | bytes 3076
  25.2 136.9 %copy-start.8 = (bf16[4,256,128]{2,1,0:T(8,128)(2,1)S(1)}, bf16[4,256,128]{2,1,0:T(8,128)(2,1)}, u32[]{:S(2)}) copy-start(bf16[4,256,128]{2,1,0:T(8,128)(2,1)} %param.7) | copy-start | bytes 786436
  25.2 156.5 %all-to-all-start = ((bf16[8,8,256,256]{3,2,1,0:T(8,128)(2,1)}), bf16[8,8,256,256]{3,2,1,0:T(8,128)(2,1)}, u32[]{:S(2)}, u32[]{:S(2)}) async-start(bf16[8,8,256,256]{3,2,1,0:T(8,128)(2,1)} %stack.74), calls=%async_computation | async-start | bytes 16777216 | tf_op jit(solution)/shard_map/all_to_all | solution.py:37
  30.3 131.8 %all-gather.2.cloned.1.call-start = ((), (), s32[]{:S(2)}) async-start(), calls=%async_computation.2 | async-start | bytes 2359296 | tf_op jit(solution)/shard_map/all_gather | solution.py:35
  31.0 587.2 %reduce-scatter.2.cloned.1.call-start = ((), (), s32[]{:S(2)}) async-start(), calls=%async_computation.3 | async-start | bytes 26738688 | tf_op jit(solution)/shard_map/reduce_scatter | solution.py:54
  31.1 103.5 %collective-permute-start.1 = (bf16[4,256]{1,0:T(4,128)(2,1)S(1)}, bf16[4,256]{1,0:T(4,128)(2,1)S(1)}, u32[]{:S(2)}, u32[]{:S(2)}) collective-permute-start(bf16[4,256]{1,0:T(4,128)(2,1)S(1)} %copy-done.9), channel_id=1, source_target_pairs={{120,0},{0,8},{8,16},{16,24},{24,32},{32,40},{40,48},{48,56},{56,6... | collective-permute-start | bytes 6152 | tf_op jit(solution)/shard_map/ppermute | solution.py:12
  162.0 6.2 copy-start
  407.7 3.5 copy-start.5
  407.7 4.1 copy-start.6
  407.7 4.7 copy-start.7
  411.1 2.1 copy-start.2
  411.1 2.7 copy-start.3
  411.1 3.3 copy-start.4
  413.2 2.0 copy-start.1
Sparse Core Ops, SparseCore 0:
  32.8 129.2 all-gather.1
  426.0 192.1 reduce-scatter.1
